TPU v7x, 128 devices: a whole 4x4x4 slice. The times are simulated.
128 devices in a mesh: cplx: 4 (over y), frag: 32 (over z, x, core).
Axes of the slice: x: 4, y: 4, z: 4, core: 2. Of those that a mesh axis runs over, the one named last changes fastest.
Arguments:
- coeffs: float32 [2048, 256], P(('cplx', 'frag')), parts along dimension 0, may hold values from -0.3 to 0.3
- centres: float32 [2048, 4, 256], P(('cplx', 'frag')), parts along dimension 0, may hold values from -3 to 3, as said below
- frag_sizes: int32 [2048], P(('cplx', 'frag')), parts along dimension 0, may hold values from 64 to 256
- pairs: int32 [131072, 2], P(('cplx', 'frag')), parts along dimension 0, may hold values from 0 to 511, as said below
Outputs:
- potential: float32 [2048, 256], P(('cplx', 'frag')), parts along dimension 0
There are 4 independent parts, one for each index of `cplx`. A program takes and returns all parts, laid end to end along the dimension named above; each array names one. Nothing has to cross between parts.
Inputs may be any that keep to these rules, and one draw needn't show every extreme that they name: `pairs`: slots 1024 * d to 1024 * (d + 1) - 1 belong to device d of frag; their first fragment is one of fragments 16 * d to 16 * (d + 1) - 1. Slot r of that block (counted from the block's start) either has its second fragment equal to its first (an empty slot) or names a second fragment owned by device r // 32, that is one of fragments 16 * (r // 32) on. Slots toward the device itself are never empty and never name the same fragment twice. `centres`: widths are positive.
All inputs are finite; a program needn't handle non-finite values.
Results may differ from a plain program's by a relative error of at most 0.0003.
Values sent between devices are 32-bit elements; how exact they have to be, the bound alone decides.
No kernel may reach another device: no remote copies, remote signals or barrier semaphores. Data moves between devices by JAX's collectives and lax.ppermute only.
A program may use at most 128 MiB of HBM per device.

v0:
```python
import functools

import jax
import jax.numpy as jnp
from jax import lax
from jax.experimental import pallas as pl
from jax.experimental.pallas import tpu as pltpu
from jax.sharding import PartitionSpec as P

FRAG_DEV = 16
AUX = 256
ROWS = 96
NF = 64
NG = 128
CHUNK = 32
CPF = AUX // CHUNK
WIDE = 4
NARROW = 8
SPAN = 96
WIDE_ROWS = 24
THIN_ROWS = 16
LIST_ROWS = WIDE_ROWS + THIN_ROWS
DUMMY = NF * CPF
DEPTH = 48
BATCH = 16
SHIFT = 3
WIDTH_FLOOR = 1.0 / 32.0


def pieces(value):
    first = value.astype(jnp.bfloat16).astype(jnp.float32)
    rest = value - first
    second = rest.astype(jnp.bfloat16).astype(jnp.float32)
    return first, second, rest - second


def pack_kernel(coeffs, centres, sizes, pairs, out):
    for k in range(4):
        out[pl.ds(16 * k, 16), :] = centres[:, k, :]
    row = sizes[...].astype(jnp.float32)
    square = (FRAG_DEV, FRAG_DEV)
    eye = lax.broadcasted_iota(jnp.int32, square, 0) == lax.broadcasted_iota(jnp.int32, square, 1)
    column = jnp.sum(jnp.where(eye, row, 0.0), axis=1, keepdims=True)
    lane = lax.broadcasted_iota(jnp.int32, (FRAG_DEV, AUX), 1).astype(jnp.float32)
    out[pl.ds(64, 16), :] = coeffs[...] * (lane < column).astype(jnp.float32)
    out[pl.ds(88, 8), :] = jnp.zeros((8, AUX), jnp.float32)
    out[pl.ds(88, 1), 0:FRAG_DEV] = row
    for r in range(8):
        out[pl.ds(80 + r, 1), :] = pairs[r // 4:r // 4 + 1, AUX * (r % 4):AUX * (r % 4) + AUX].astype(jnp.float32)


def pair_kernel(*refs):
    sources, refs = refs[:11], refs[11:]
    out_far, out_near, out_own, outf_far, outf_near, outf_own = refs[:6]
    (lhs, rows_c, rows_s, cols_s, cols_c, rhs, build, slots, counts, chunks, zeros_v, places, ends,
     table_v, tiles_v, row_sums, table, tile_list, sem) = refs[6:25]
    packets, arrived = refs[25:36], refs[36]
    loads = [pltpu.make_async_copy(a, b, arrived.at[k]) for k, (a, b) in enumerate(zip(sources, packets))]
    for load in loads:
        load.start()
    f_blocks = [packets[0], packets[1], packets[2], packets[3]]
    g_blocks = [packets[0]] + list(packets[4:])
    me = lax.axis_index("frag")
    plane, column = lax.div(me, 8), lax.rem(me, 8)
    zs = [plane, plane ^ 1, 3 - plane, (3 - plane) ^ 1]
    f_devs = [8 * at + column for at in zs]
    line, core = lax.div(column, 2), lax.rem(column, 2)
    xs = [line, line ^ 1, 3 - line, (3 - line) ^ 1]
    g_devs = [8 * plane + 2 * at + c for c in (core, 1 - core) for at in xs]

    def put_rows(r, value):
        for h in range(2):
            build[h, pl.ds(r * 16, 16), :] = value[:, 128 * h:128 * h + 128]

    def take_rows(h, at, count):
        return build.at[h][pl.ds(at, count, stride=16), :]

    lowest = None
    for i, blk in enumerate(f_blocks):
        loads[i].wait()
        x, y, z, w, c = (blk[pl.ds(16 * k, 16), :] for k in range(5))
        lowest = w if lowest is None else jnp.minimum(lowest, w)
        s = x * x + y * y + z * z + w
        one = jnp.ones_like(x)
        zero = jnp.zeros_like(x)
        px, py, pz = pieces(-2.0 * x), pieces(-2.0 * y), pieces(-2.0 * z)
        ps, pw, pc = pieces(s), pieces(w), pieces(c)
        for k in range(3):
            delta = one if k == 0 else zero
            extra = pc if k == 0 else (pw if k == 1 else (zero, zero, zero))
            rows = [px[k], py[k], pz[k], delta, ps[k], *extra,
                    px[k], py[k], pz[k], delta, px[k], py[k], pz[k], delta]
            for r, value in enumerate(rows):
                put_rows(16 * k + r, value)

        def one_row(lf, _, i=i):
            for h in range(2):
                feats = take_rows(h, lf, DEPTH).T
                feats = jnp.concatenate([feats, jnp.zeros((128, 128 - DEPTH), jnp.float32)], axis=1)
                lhs[pl.ds((i * 16 + lf) * CPF + 4 * h, 4), 0:CHUNK, :] = feats.astype(jnp.bfloat16).reshape(4, CHUNK, 128)
            return 0

        lax.fori_loop(0, 16, one_row, 0, unroll=16)
    spare_lane = lax.broadcasted_iota(jnp.int32, (CHUNK, 128), 1)
    lhs[DUMMY, 0:CHUNK, :] = (spare_lane == 4).astype(jnp.float32).astype(jnp.bfloat16)

    pick = lax.broadcasted_iota(jnp.int32, (128, 128), 0)

    def spread(rows, lo, hi, scale):
        sel = jnp.where((pick >= lo) & (pick <= hi), scale, 0.0)
        return jnp.dot(rows, sel.astype(jnp.bfloat16), preferred_element_type=jnp.float32)

    def one_spread(f, _):
        value = spread(lhs[pl.ds(f * CPF, CPF), 0:CHUNK, :].reshape(AUX, 128), 5, 7, 1.0)
        rows_c[pl.ds(f * CPF, CPF)] = value.reshape(CPF, CHUNK, 128)
        rows_s[pl.ds(f * CPF, CPF)] = jnp.zeros((CPF, CHUNK, 128), jnp.float32)
        return 0

    lax.fori_loop(0, NF, one_spread, 0, unroll=16)
    rows_c[DUMMY] = jnp.zeros((CHUNK, 128), jnp.float32)
    rows_s[DUMMY] = jnp.zeros((CHUNK, 128), jnp.float32)

    for load in loads[4:]:
        load.wait()
    for j, blk in enumerate(g_blocks):
        x, y, z, w, c = (blk[pl.ds(16 * k, 16), :] for k in range(5))
        lowest = jnp.minimum(lowest, w)
        s = x * x + y * y + z * z + w
        one = jnp.ones_like(x)
        zero = jnp.zeros_like(x)
        px, py, pz, ps = pieces(x), pieces(y), pieces(z), pieces(s)
        rows = [px[0], py[0], pz[0], ps[0], one, zero, zero, zero,
                px[1], py[1], pz[1], ps[1], px[2], py[2], pz[2], ps[2]]
        for r, value in enumerate(rows):
            put_rows(r, value)

        def one_column(lg, _, j=j, blk=blk):
            cols_s[j * 16 + lg] = jnp.zeros((16, 128), jnp.float32)
            coef = blk[pl.ds(64 + lg, 1), :]
            for h in range(2):
                cols_c[j * 16 + lg, h:h + 1, :] = coef[:, 128 * h:128 * h + 128]
            rhs[j * 16 + lg] = jnp.concatenate([take_rows(h, lg, 16) for h in range(2)], axis=1).astype(jnp.bfloat16)
            return 0

        lax.fori_loop(0, 16, one_column, 0, unroll=16)

    lane = lax.broadcasted_iota(jnp.int32, (8, AUX), 1)
    back = jnp.zeros((8, AUX), jnp.float32)
    for j, blk in enumerate(g_blocks):
        shift = lax.rem(32 * j - 32 * column + 256, 256)
        turned = pltpu.roll(blk[pl.ds(80, 8), :], shift, 1)
        back = jnp.where(lane // 32 == j, turned, back)
    slots[...] = back
    g_lane = lax.broadcasted_iota(jnp.int32, (16, AUX), 0).astype(jnp.float32)
    g_ids = jnp.concatenate([g_lane + (16 * g_devs[j]).astype(jnp.float32) for j in range(8)], axis=0)
    for i, blk in enumerate(f_blocks):
        f_ids = g_lane + (16 * f_devs[i]).astype(jnp.float32)
        f_plane = zs[i]

        def table_of(row_f, row_g):
            odd = (row_f + row_g) - 2.0 * jnp.floor((row_f + row_g) * 0.5)
            less = (row_f < row_g).astype(jnp.float32)
            use = (odd == less) & (row_f != row_g)
            row_f = jnp.where(use, row_f, -1.0)
            left = (row_f == f_ids).astype(jnp.float32).astype(jnp.bfloat16)
            right = (row_g == g_ids).astype(jnp.float32).astype(jnp.bfloat16)
            return lax.dot_general(left, right, (((1,), (1,)), ((), ())), preferred_element_type=jnp.float32)

        there = table_of(blk[pl.ds(80 + plane, 1), :], blk[pl.ds(84 + plane, 1), :])
        back_i = table_of(slots[pl.ds(4 + f_plane, 1), :], slots[pl.ds(f_plane, 1), :])
        counts[pl.ds(16 * i, 16), :] = there + back_i
        sizes = blk[pl.ds(88, 1), :]
        eye = lax.broadcasted_iota(jnp.int32, (16, AUX), 0) == lax.broadcasted_iota(jnp.int32, (16, AUX), 1)
        size_col = jnp.sum(jnp.where(eye, sizes, 0.0), axis=1, keepdims=True)
        many = jnp.floor((size_col + (CHUNK - 1)) * (1.0 / CHUNK))
        chunks[pl.ds(16 * i, 16), :] = jnp.broadcast_to(many, (16, 128))

    most = jnp.max(counts[...]).astype(jnp.int32)
    safe = jnp.min(lowest) >= WIDTH_FLOOR
    row8 = lax.broadcasted_iota(jnp.int32, (8, 128), 0)

    lane8 = lax.broadcasted_iota(jnp.int32, (8, 128), 1)
    sizes = jnp.zeros((8, 128), jnp.float32)
    for j, blk in enumerate(g_blocks):
        part = blk[pl.ds(88, 8), 0:128]
        part = part if j == 0 else pltpu.roll(part, 16 * j, 1)
        sizes = jnp.where(lane8 // 16 == j, part, sizes)
    slots[:, 0:128] = sizes
    is_wide = jnp.where(jnp.broadcast_to(slots[pl.ds(0, 1), 0:128], (8, 128)) > 128.0, 1.0, 0.0)
    per_tile = jnp.where(is_wide > 0.0, float(WIDE), float(NARROW))
    contract = (((1,), (1,)), ((), ()))

    blank = jnp.zeros((128 - DEPTH, 128), jnp.bfloat16)
    none = jnp.zeros((128, 128), jnp.bfloat16)

    def chunks_of(code, take):
        g, q = code & 127, code >> 7
        views = [table.at[q + v, :, pl.ds(g, 1)] for v in range(take // WIDE)]
        at = [views[u // WIDE][u % WIDE, 0] for u in range(take)]
        times = at[0] >> 10
        return g, times, [e & 1023 if u % WIDE == 0 else e for u, e in enumerate(at)]

    def distances(g, at, kind):
        block = rhs[g]
        left = jnp.concatenate([lhs[e, 0:CHUNK, :] for e in at[:4]], axis=0)
        if kind == "narrow":
            left = jnp.concatenate([left, jnp.concatenate([lhs[e, 0:CHUNK, :] for e in at[4:]], axis=0)], axis=1)
            thin = block[:, :128]
            right = jnp.concatenate([thin, thin, thin, blank], axis=0)
            right = jnp.concatenate([jnp.concatenate([right, none], axis=1), jnp.concatenate([none, right], axis=1)], axis=0)
        else:
            right = jnp.concatenate([block, block, block, jnp.concatenate([blank, blank], axis=1)], axis=0)
        return jnp.dot(left, right, preferred_element_type=jnp.float32)

    def gather(at):
        return jnp.concatenate([rows_c[e] for e in at], axis=0)

    def fold(value):
        return jnp.sum(value.reshape(-1, 8, 128), axis=0)

    def apply(kern, kind, g, times, at):
        times = times.astype(jnp.float32)
        k0, k1 = kern[:, :128], kern[:, 128:]
        weight = cols_c[g, 0:1, :] * times
        if kind == "narrow":
            second = fold(k0 * gather(at[:4]) + k1 * gather(at[4:]))
            cols_s[g, 0:8, :] = cols_s[g, 0:8, :] + second * times
            first = [k[u * CHUNK:(u + 1) * CHUNK] * weight for k in (k0, k1) for u in range(4)]
        else:
            coef = gather(at)
            cols_s[g, 0:8, :] = cols_s[g, 0:8, :] + fold(k0 * coef) * times
            cols_s[g, 8:16, :] = cols_s[g, 8:16, :] + fold(k1 * coef) * times
            both = k0 * weight + k1 * (cols_c[g, 1:2, :] * times)
            first = [both[u * CHUNK:(u + 1) * CHUNK] for u in range(4)]
        sums = [rows_s[e] for e in at]
        for e, value, more in zip(at, sums, first):
            rows_s[e] = value + more

    def exact(code):
        g, times, at = chunks_of(code, WIDE)
        left = jnp.concatenate([lhs[e, 0:CHUNK, :] for e in at], axis=0)
        part = rhs[g].astype(jnp.float32)
        wide = spread(left, 21, 23, 1.0)
        dist = jnp.concatenate([wide, wide], axis=1) + width_row(g)
        for k in range(3):
            mine = jnp.where(((pick % 16 == k) & (pick < DEPTH)), -0.5, 0.0).astype(jnp.bfloat16)
            mine = jnp.dot(left, mine, preferred_element_type=jnp.float32)
            other = part[k:k + 1] + part[8 + k:9 + k] + part[12 + k:13 + k]
            gap = jnp.concatenate([mine, mine], axis=1) - other
            dist = dist + gap * gap
        apply(lax.rsqrt(dist), "wide", g, times, at)

    def width_row(g):
        row = jnp.zeros((1, AUX), jnp.float32)
        for k, blk in enumerate(g_blocks):
            row = jnp.where(g // 16 == k, blk[pl.ds(48 + g % 16, 1), :], row)
        return row

    def one_round(state):
        r, _ = state
        groups = SPAN // 8
        at = [(row8 + 8 * t + SPAN * r).astype(jnp.float32) for t in range(groups)]

        def one_class(m, state):
            vals, times, total = state
            times = tuple(jnp.where(a >= total, m.astype(jnp.float32), v) for a, v in zip(at, times))

            def scan(f, state):
                vals, total = state
                many = jnp.broadcast_to(chunks[pl.ds(f, 1), :], (8, 128))
                listed = jnp.broadcast_to(counts[pl.ds(f, 1), :], (8, 128))
                mark = (many + f.astype(jnp.float32) * 16.0) * 4096.0 + total
                vals = tuple(jnp.where(a >= total, mark, v) for a, v in zip(at, vals))
                return vals, total + jnp.where(listed == m.astype(jnp.float32), many, 0.0)

            vals, total = lax.fori_loop(0, NF, scan, (vals, total), unroll=8)
            vals = tuple(jnp.where(a >= total, -1.0, v) for a, v in zip(at, vals))
            total = jnp.floor((total + per_tile - 1.0) / per_tile) * per_tile
            return vals, times, total

        flat = zeros_v[...]
        none = (flat,) * groups
        vals, times, total = lax.fori_loop(1, most + 1, one_class, (none, none, flat))
        for t in range(groups):
            code = jnp.floor(vals[t] * (1.0 / 4096.0))
            offset = at[t] - (vals[t] - 4096.0 * code)
            frag = jnp.floor(code * (1.0 / 16.0))
            entry = jnp.where((vals[t] >= 0.0) & (at[t] < total), frag * CPF + offset, float(DUMMY))
            places[0, pl.ds(8 * t, 8), :] = entry
            places[1, pl.ds(8 * t, 8), :] = times[t]
        groups4 = SPAN // WIDE
        for u in range(WIDE):
            value = places.at[0][pl.ds(u, groups4, stride=WIDE), :]
            if u == 0:
                value = value + 1024.0 * places.at[1][pl.ds(u, groups4, stride=WIDE), :]
            table_v[pl.ds(0, groups4), u, :] = value.astype(jnp.int32)
        table_v[pl.ds(groups4, 2)] = jnp.full((2, WIDE, 128), DUMMY, jnp.int32)
        left_over = jnp.clip(total - (SPAN * r).astype(jnp.float32), 0.0, float(SPAN))
        tiles = left_over / per_tile
        tiles_wide = tiles * is_wide
        tiles_thin = tiles - tiles_wide
        for k, tiles in enumerate((tiles_wide, tiles_thin)):
            ends[k] = lax.dot_general(upto, jnp.concatenate([tiles] * 16, axis=0).astype(jnp.bfloat16), contract, preferred_element_type=jnp.float32)
        number = [(lane8 + 128 * row8 + 1024 * k).astype(jnp.float32) for k in range(WIDE_ROWS // 8)]
        kinds = [(0, k) for k in range(WIDE_ROWS // 8)] + [(1, k) for k in range(THIN_ROWS // 8)]

        def seek(c, state):
            out = []
            column = (c + 1).astype(jnp.float32)
            edges = [jnp.broadcast_to(ends.at[n][pl.ds(c, 1), :], (8, 128)) for n in range(2)]
            for (thin, k), (where, begin) in zip(kinds, state):
                end = edges[thin]
                hit = number[k] >= end
                out.append((jnp.where(hit, column, where), jnp.where(hit, end, begin)))
            return tuple(out)

        found = lax.fori_loop(0, NG, seek, ((flat, flat),) * len(kinds), unroll=16)
        for (thin, k), (where, begin) in zip(kinds, found):
            place = (number[k] - begin) * (128.0 * (1 + thin)) + where
            place = jnp.where(where < float(NG), place, float(groups4 * 128))
            tiles_v[pl.ds(thin * WIDE_ROWS + 8 * k, 8), :] = place.astype(jnp.int32)
        info = jnp.where(row8 == 0, jnp.sum(tiles_wide, axis=1, keepdims=True), jnp.sum(tiles_thin, axis=1, keepdims=True))
        tiles_v[pl.ds(LIST_ROWS, 8), :] = info.astype(jnp.int32)
        longest = jnp.max(total).astype(jnp.int32)
        copies = [pltpu.make_async_copy(table_v, table, sem.at[0]), pltpu.make_async_copy(tiles_v, tile_list, sem.at[1])]
        for copy in copies:
            copy.start()
        for copy in copies:
            copy.wait()
        count_wide, count_thin = tile_list[LIST_ROWS, 0], tile_list[LIST_ROWS + 1, 0]

        def many_tiles(kind, first_row, count):
            take = NARROW if kind == "narrow" else WIDE

            def body(b, _):
                row, col = first_row + lax.shift_right_logical(b, SHIFT), (b & (128 // BATCH - 1)) * BATCH
                for u in range(BATCH):
                    g, times, at = chunks_of(tile_list[row, col + u], take)
                    apply(lax.rsqrt(distances(g, at, kind)), kind, g, times, at)
                return 0

            lax.fori_loop(0, (count + (BATCH - 1)) // BATCH, body, 0)

        @pl.when(safe)
        def _():
            many_tiles("wide", 0, count_wide)
            many_tiles("narrow", WIDE_ROWS, count_thin)

        @pl.when(jnp.logical_not(safe))
        def _():
            def wide_one(t, _):
                exact(tile_list[t >> 7, t & 127])
                return 0

            def thin_one(t, _):
                exact(tile_list[WIDE_ROWS + (t >> 8), (t & 255) >> 1] + 128 * (t & 1))
                return 0

            lax.fori_loop(0, count_wide, wide_one, 0)
            lax.fori_loop(0, 2 * count_thin, thin_one, 0)

        return r + 1, longest

    zeros_v[...] = jnp.zeros_like(zeros_v)
    upto = (lax.broadcasted_iota(jnp.int32, (128, 128), 1) <= pick).astype(jnp.float32).astype(jnp.bfloat16)
    lax.while_loop(lambda state: state[0] * SPAN < state[1], one_round, (jnp.int32(0), jnp.int32(1)))

    ones8 = jnp.ones((8, 256), jnp.bfloat16)

    def collect(f, _):
        value = rows_s[pl.ds(f * CPF, CPF)].reshape(AUX, 128)
        high = value.astype(jnp.bfloat16)
        low = (value - high.astype(jnp.float32)).astype(jnp.bfloat16)
        row = lax.dot_general(ones8, jnp.concatenate([high, low], axis=1), contract, preferred_element_type=jnp.float32)
        for h in range(2):
            row_sums[h, pl.ds(f, 1), :] = row[0:1, 128 * h:128 * h + 128]
        return 0

    lax.fori_loop(0, NF, collect, 0, unroll=16)
    rows_out = jnp.concatenate([row_sums[0], row_sums[1]], axis=1)
    outf_own[...] = rows_out[0:16]
    outf_near[...] = rows_out[16:32]
    outf_far[...] = rows_out[32:64]
    cols = []
    for h in range(2):
        flat_s = cols_s.reshape(NG * 16, 128)
        half = flat_s[pl.ds(8 * h, NG, stride=16), :]
        for r in range(1, 8):
            half = half + flat_s[pl.ds(8 * h + r, NG, stride=16), :]
        cols.append(half)
    cols = jnp.concatenate(cols, axis=1)
    for k in range(2):
        part = pl.ds(16 * k, 16)
        out_own[part, :] = cols[64 * k:64 * k + 16]
        out_near[part, :] = cols[64 * k + 16:64 * k + 32]
        out_far[part, :] = cols[64 * k + 32:64 * k + 48]
        out_far[pl.ds(32 + 16 * k, 16), :] = cols[64 * k + 48:64 * k + 64]


def rectangle(packets):
    vmem = pl.BlockSpec(memory_space=pltpu.VMEM)
    shape = lambda rows: jax.ShapeDtypeStruct((rows, AUX), jnp.float32)
    return pl.pallas_call(
        pair_kernel,
        out_shape=(shape(64), shape(32), shape(32), shape(32), shape(16), shape(16)),
        in_specs=[pl.BlockSpec(memory_space=pl.ANY)] * 11,
        out_specs=(vmem,) * 6,
        scratch_shapes=[
            pltpu.VMEM((DUMMY + 1, 2 * CHUNK, 128), jnp.bfloat16),
            pltpu.VMEM((DUMMY + 1, CHUNK, 128), jnp.float32),
            pltpu.VMEM((DUMMY + 1, CHUNK, 128), jnp.float32),
            pltpu.VMEM((NG, 16, 128), jnp.float32),
            pltpu.VMEM((NG, 16, 128), jnp.float32),
            pltpu.VMEM((NG, 16, AUX), jnp.bfloat16),
            pltpu.VMEM((2, DEPTH * 16, 128), jnp.float32),
            pltpu.VMEM((8, AUX), jnp.float32),
            pltpu.VMEM((NF, 128), jnp.float32),
            pltpu.VMEM((NF, 128), jnp.float32),
            pltpu.VMEM((8, 128), jnp.float32),
            pltpu.VMEM((2, SPAN, 128), jnp.float32),
            pltpu.VMEM((2, 128, 128), jnp.float32),
            pltpu.VMEM((SPAN // WIDE + 2, WIDE, 128), jnp.int32),
            pltpu.VMEM((LIST_ROWS + 8, 128), jnp.int32),
            pltpu.VMEM((2, NF, 128), jnp.float32),
            pltpu.SMEM((SPAN // WIDE + 2, WIDE, 128), jnp.int32),
            pltpu.SMEM((LIST_ROWS + 8, 128), jnp.int32),
            pltpu.SemaphoreType.DMA((2,)),
        ]
        + [pltpu.VMEM((ROWS, AUX), jnp.float32)] * 11
        + [
            pltpu.SemaphoreType.DMA((11,)),
        ],
        compiler_params=pltpu.CompilerParams(vmem_limit_bytes=56 * 2**20),
    )(*packets)


def index_of(z, x, c):
    return (z * 4 + x) * 2 + c


def partners(move):
    return [
        (index_of(z, x, c), index_of(*move(z, x, c)))
        for z in range(4) for x in range(4) for c in range(2)
    ]


X_NEAR = partners(lambda z, x, c: (z, x ^ 1, c))
X_FAR = partners(lambda z, x, c: (z, 3 - x, c))
Z_NEAR = partners(lambda z, x, c: (z ^ 1, x, c))
Z_FAR = partners(lambda z, x, c: (3 - z, x, c))
X_LAST = partners(lambda z, x, c: (z, x ^ 2, c))
Z_LAST = partners(lambda z, x, c: (z ^ 2, x, c))
CORE = partners(lambda z, x, c: (z, x, c ^ 1))


def swap(array, pairs):
    return lax.ppermute(array, "frag", pairs)


def local(coeffs, centres, frag_sizes, pairs):
    mask = (jnp.arange(AUX, dtype=jnp.int32)[None, :] < frag_sizes[:, None]).astype(jnp.float32)
    vmem = pl.BlockSpec(memory_space=pltpu.VMEM)
    packet = pl.pallas_call(
        pack_kernel,
        out_shape=jax.ShapeDtypeStruct((ROWS, AUX), jnp.float32),
        in_specs=[vmem] * 4,
        out_specs=vmem,
    )(coeffs, centres, frag_sizes.reshape(1, FRAG_DEV), pairs.T)

    x_near = swap(packet, X_NEAR)
    x_far = swap(packet, X_FAR)
    x_last = swap(packet, X_LAST)
    z_near = swap(packet, Z_NEAR)
    z_far = swap(packet, Z_FAR)
    z_last = swap(packet, Z_LAST)
    own_c = swap(packet, CORE)
    near_c = swap(x_near, CORE)
    far_c = swap(x_far, CORE)
    last_c = swap(x_last, CORE)

    g_far, g_near, g_own, f_far, f_near, f_own = rectangle(
        (packet, z_near, z_far, z_last, x_near, x_far, x_last, own_c, near_c, far_c, last_c),
    )
    far_back = swap(g_far, X_FAR)
    f_back = swap(f_far, Z_FAR)
    near_back = swap(g_near + far_back[32:], X_NEAR)
    f_last = swap(f_near + f_back[16:], Z_NEAR)
    both = g_own + far_back[:32] + near_back
    total = both[:16] + f_own + f_back[:16] + f_last + swap(both[16:], CORE)
    return total * mask


def solution(mesh):
    return jax.shard_map(
        local,
        mesh=mesh,
        in_specs=(
            P(("cplx", "frag"), None),
            P(("cplx", "frag"), None, None),
            P(("cplx", "frag")),
            P(("cplx", "frag"), None),
        ),
        out_specs=P(("cplx", "frag"), None),
        check_vma=False,
    )
```

profile of v0, /device:TPU:25, one launch (start us, length us, event | category | flops | bytes accessed | tf_op | source)
XLA Modules:
  0.0 241.6 jit_solution(2471972125432535446)
XLA Ops:
  0.0 1.6 shard_map.46.refs_0_
  1.6 0.7 collective-permute-start.6
  2.2 2.7 %collective-permute-start.5 = (f32[96,256]{1,0:T(8,128)}, f32[96,256]{1,0:T(8,128)S(1)}, u32[]{:S(2)}, u32[]{:S(2)}) collective-permute-start(f32[96,256]{1,0:T(8,128)} %shard_map.46.refs_0_), channel_id=1, source_target_pairs={{0,4},{1,5},{2,6},{3,7},{4,0},{5,1},{6,2},{7,3},{8,12},{9,13},{10,... | collective-permute-start | bytes 294920 | tf_op jit(solution)/shard_map/ppermute | solution.py:458
  5.0 0.9 collective-permute-start.4
  5.8 3.6 %collective-permute-start.2 = (f32[96,256]{1,0:T(8,128)}, f32[96,256]{1,0:T(8,128)S(1)}, u32[]{:S(2)}, u32[]{:S(2)}) collective-permute-start(f32[96,256]{1,0:T(8,128)} %shard_map.46.refs_0_), channel_id=1, source_target_pairs={{0,16},{1,17},{2,18},{3,19},{4,20},{5,21},{6,22},{7,23},{8,24},{9,... | collective-permute-start | bytes 294920 | tf_op jit(solution)/shard_map/ppermute | solution.py:458
  9.4 0.4 collective-permute-start.1
  9.9 0.4 collective-permute-start
  10.3 0.2 collective-permute-done.4.refs_5_
  10.5 1.1 collective-permute-start.9
  11.6 0.1 collective-permute-start.8
  11.7 0.6 collective-permute-done.2.refs_3_
  12.4 1.4 collective-permute-start.7
  13.8 0.9 collective-permute-done.1.refs_2_
  14.7 0.3 collective-permute-done.refs_1_
  15.0 0.3 copy-done.5
  15.3 0.3 copy-done.6
  15.6 0.6 copy-done.9
  16.3 206.7 %shard_map.47 = (f32[64,256]{1,0:T(8,128)}, f32[32,256]{1,0:T(8,128)}, f32[32,256]{1,0:T(8,128)}, f32[32,256]{1,0:T(8,128)}, f32[16,256]{1,0:T(8,128)}, /*index=5*/f32[16,256]{1,0:T(8,128)}) custom-call(f32[96,256]{1,0:T(8,128)} %shard_map.46.refs_0_, f32[96,256]{1,0:T(8,128)} %copy-done.6, f32[96,256]{1,0:T(8,128)} %copy-done.5, f32[96,256]{1,0:T(8,128)} %copy-done.4, ...), custom_call_target="tpu_custom_call" | custom-call | tf_op jit(solution)/shard_map/pallas_call | solution.py:403
  223.2 4.5 %collective-permute-done.10 = f32[64,256]{1,0:T(8,128)S(1)} collective-permute-done((f32[64,256]{1,0:T(8,128)}, f32[64,256]{1,0:T(8,128)S(1)}, u32[]{:S(2)}, u32[]{:S(2)}) %collective-permute-start.10) | collective-permute-done | bytes 65568 | tf_op jit(solution)/shard_map/ppermute | solution.py:458
  227.7 0.8 slice_add_fusion
  228.5 3.9 %collective-permute-start.13 = (f32[16,256]{1,0:T(8,128)S(1)}, f32[16,256]{1,0:T(8,128)S(1)}, u32[]{:S(2)}, u32[]{:S(2)}) collective-permute-start(f32[16,256]{1,0:T(8,128)S(1)} %slice_add_fusion.2), channel_id=1, source_target_pairs={{0,8},{1,9},{2,10},{3,11},{4,12},{5,13},{6,14},{7,15},{8,0},{9,1},... | collective-permute-start | bytes 49160 | tf_op jit(solution)/shard_map/ppermute | solution.py:458
  232.5 7.6 %collective-permute-start.14 = (f32[16,256]{1,0:T(8,128)S(1)}, f32[16,256]{1,0:T(8,128)S(1)}, u32[]{:S(2)}, u32[]{:S(2)}) collective-permute-start(f32[16,256]{1,0:T(8,128)S(1)} %slice.29), channel_id=1, source_target_pairs={{0,1},{1,0},{2,3},{3,2},{4,5},{5,4},{6,7},{7,6},{8,9},{9,8},{10,11... | collective-permute-start | bytes 49160 | tf_op jit(solution)/shard_map/ppermute | solution.py:458
  240.1 0.8 collective-permute-done.14
  241.0 0.7 fusion.3
  (41 shorter events, 0.3 us)
Async XLA Ops:
  1.6 7.9 %collective-permute-start.6 = (f32[96,256]{1,0:T(8,128)}, f32[96,256]{1,0:T(8,128)S(1)}, u32[]{:S(2)}, u32[]{:S(2)}) collective-permute-start(f32[96,256]{1,0:T(8,128)} %shard_map.46.refs_0_), channel_id=1, source_target_pairs={{0,1},{1,0},{2,3},{3,2},{4,5},{5,4},{6,7},{7,6},{8,9},{9,8},{10,11... | collective-permute-start | bytes 294920 | tf_op jit(solution)/shard_map/ppermute | solution.py:458
  2.2 7.6 %collective-permute-start.5 = (f32[96,256]{1,0:T(8,128)}, f32[96,256]{1,0:T(8,128)S(1)}, u32[]{:S(2)}, u32[]{:S(2)}) collective-permute-start(f32[96,256]{1,0:T(8,128)} %shard_map.46.refs_0_), channel_id=1, source_target_pairs={{0,4},{1,5},{2,6},{3,7},{4,0},{5,1},{6,2},{7,3},{8,12},{9,13},{10,... | collective-permute-start | bytes 294920 | tf_op jit(solution)/shard_map/ppermute | solution.py:458
  5.0 5.5 %collective-permute-start.4 = (f32[96,256]{1,0:T(8,128)}, f32[96,256]{1,0:T(8,128)S(1)}, u32[]{:S(2)}, u32[]{:S(2)}) collective-permute-start(f32[96,256]{1,0:T(8,128)} %shard_map.46.refs_0_), channel_id=1, source_target_pairs={{0,6},{1,7},{2,4},{3,5},{4,2},{5,3},{6,0},{7,1},{8,14},{9,15},{10,... | collective-permute-start | bytes 294920 | tf_op jit(solution)/shard_map/ppermute | solution.py:458
  5.8 5.8 %collective-permute-start.3 = (f32[96,256]{1,0:T(8,128)}, f32[96,256]{1,0:T(8,128)S(1)}, u32[]{:S(2)}, u32[]{:S(2)}) collective-permute-start(f32[96,256]{1,0:T(8,128)} %shard_map.46.refs_0_), channel_id=1, source_target_pairs={{0,2},{1,3},{2,0},{3,1},{4,6},{5,7},{6,4},{7,5},{8,10},{9,11},{10,... | collective-permute-start | bytes 294920 | tf_op jit(solution)/shard_map/ppermute | solution.py:458
  5.8 6.5 %collective-permute-start.2 = (f32[96,256]{1,0:T(8,128)}, f32[96,256]{1,0:T(8,128)S(1)}, u32[]{:S(2)}, u32[]{:S(2)}) collective-permute-start(f32[96,256]{1,0:T(8,128)} %shard_map.46.refs_0_), channel_id=1, source_target_pairs={{0,16},{1,17},{2,18},{3,19},{4,20},{5,21},{6,22},{7,23},{8,24},{9,... | collective-permute-start | bytes 294920 | tf_op jit(solution)/shard_map/ppermute | solution.py:458
  9.4 5.5 %copy-start = (f32[96,256]{1,0:T(8,128)}, f32[96,256]{1,0:T(8,128)S(1)}, u32[]{:S(2)}) copy-start(f32[96,256]{1,0:T(8,128)S(1)} %collective-permute-done.6.refs_7_) | copy-start | bytes 294916
  9.4 5.2 %collective-permute-start.1 = (f32[96,256]{1,0:T(8,128)}, f32[96,256]{1,0:T(8,128)S(1)}, u32[]{:S(2)}, u32[]{:S(2)}) collective-permute-start(f32[96,256]{1,0:T(8,128)} %shard_map.46.refs_0_), channel_id=1, source_target_pairs={{0,24},{1,25},{2,26},{3,27},{4,28},{5,29},{6,30},{7,31},{8,16},{9,... | collective-permute-start | bytes 294920 | tf_op jit(solution)/shard_map/ppermute | solution.py:458
  9.9 5.1 %copy-start.1 = (f32[96,256]{1,0:T(8,128)}, f32[96,256]{1,0:T(8,128)S(1)}, u32[]{:S(2)}) copy-start(f32[96,256]{1,0:T(8,128)S(1)} %collective-permute-done.5.refs_6_) | copy-start | bytes 294916
  9.9 5.0 %collective-permute-start = (f32[96,256]{1,0:T(8,128)}, f32[96,256]{1,0:T(8,128)S(1)}, u32[]{:S(2)}, u32[]{:S(2)}) collective-permute-start(f32[96,256]{1,0:T(8,128)} %shard_map.46.refs_0_), channel_id=1, source_target_pairs={{0,8},{1,9},{2,10},{3,11},{4,12},{5,13},{6,14},{7,15},{8,0},{9,1},... | collective-permute-start | bytes 294920 | tf_op jit(solution)/shard_map/ppermute | solution.py:458
  10.5 4.5 %copy-start.2 = (f32[96,256]{1,0:T(8,128)}, f32[96,256]{1,0:T(8,128)S(1)}, u32[]{:S(2)}) copy-start(f32[96,256]{1,0:T(8,128)S(1)} %collective-permute-done.4.refs_5_) | copy-start | bytes 294916
  10.5 4.4 %collective-permute-start.9 = (f32[96,256]{1,0:T(8,128)S(1)}, f32[96,256]{1,0:T(8,128)S(1)}, u32[]{:S(2)}, u32[]{:S(2)}) collective-permute-start(f32[96,256]{1,0:T(8,128)S(1)} %collective-permute-done.5.refs_6_), channel_id=1, source_target_pairs={{0,1},{1,0},{2,3},{3,2},{4,5},{5,4},{6,7},{7,6},{8,9},{9,8},{10,11... | collective-permute-start | bytes 294920 | tf_op jit(solution)/shard_map/ppermute | solution.py:458
  11.6 3.4 %copy-start.3 = (f32[96,256]{1,0:T(8,128)}, f32[96,256]{1,0:T(8,128)S(1)}, u32[]{:S(2)}) copy-start(f32[96,256]{1,0:T(8,128)S(1)} %collective-permute-done.3.refs_4_) | copy-start | bytes 294916
  11.6 3.3 %collective-permute-start.8 = (f32[96,256]{1,0:T(8,128)S(1)}, f32[96,256]{1,0:T(8,128)S(1)}, u32[]{:S(2)}, u32[]{:S(2)}) collective-permute-start(f32[96,256]{1,0:T(8,128)S(1)} %collective-permute-done.4.refs_5_), channel_id=1, source_target_pairs={{0,1},{1,0},{2,3},{3,2},{4,5},{5,4},{6,7},{7,6},{8,9},{9,8},{10,11... | collective-permute-start | bytes 294920 | tf_op jit(solution)/shard_map/ppermute | solution.py:458
  12.4 2.6 %copy-start.4 = (f32[96,256]{1,0:T(8,128)}, f32[96,256]{1,0:T(8,128)S(1)}, u32[]{:S(2)}) copy-start(f32[96,256]{1,0:T(8,128)S(1)} %collective-permute-done.2.refs_3_) | copy-start | bytes 294916
  12.4 2.6 %collective-permute-start.7 = (f32[96,256]{1,0:T(8,128)S(1)}, f32[96,256]{1,0:T(8,128)S(1)}, u32[]{:S(2)}, u32[]{:S(2)}) collective-permute-start(f32[96,256]{1,0:T(8,128)S(1)} %collective-permute-done.3.refs_4_), channel_id=1, source_target_pairs={{0,1},{1,0},{2,3},{3,2},{4,5},{5,4},{6,7},{7,6},{8,9},{9,8},{10,11... | collective-permute-start | bytes 294920 | tf_op jit(solution)/shard_map/ppermute | solution.py:458
  223.0 4.7 %collective-permute-start.10 = (f32[64,256]{1,0:T(8,128)}, f32[64,256]{1,0:T(8,128)S(1)}, u32[]{:S(2)}, u32[]{:S(2)}) collective-permute-start(f32[64,256]{1,0:T(8,128)} %get-tuple-element.12), channel_id=1, source_target_pairs={{0,6},{1,7},{2,4},{3,5},{4,2},{5,3},{6,0},{7,1},{8,14},{9,15},{10,... | collective-permute-start | bytes 196616 | tf_op jit(solution)/shard_map/ppermute | solution.py:458
  223.1 5.4 %collective-permute-start.12 = (f32[32,256]{1,0:T(8,128)}, f32[32,256]{1,0:T(8,128)S(1)}, u32[]{:S(2)}, u32[]{:S(2)}) collective-permute-start(f32[32,256]{1,0:T(8,128)} %get-tuple-element.15), channel_id=1, source_target_pairs={{0,24},{1,25},{2,26},{3,27},{4,28},{5,29},{6,30},{7,31},{8,16},{9,... | collective-permute-start | bytes 98312 | tf_op jit(solution)/shard_map/ppermute | solution.py:458
  227.7 0.8 copy-start.11
  228.5 3.9 %copy-start.10 = (f32[32,256]{1,0:T(8,128)S(1)}, f32[32,256]{1,0:T(8,128)}, u32[]{:S(2)}) copy-start(f32[32,256]{1,0:T(8,128)} %get-tuple-element.11) | copy-start | bytes 98308
  228.5 3.9 %collective-permute-start.11 = (f32[32,256]{1,0:T(8,128)S(1)}, f32[32,256]{1,0:T(8,128)S(1)}, u32[]{:S(2)}, u32[]{:S(2)}) collective-permute-start(f32[32,256]{1,0:T(8,128)S(1)} %slice_add_fusion), channel_id=1, source_target_pairs={{0,2},{1,3},{2,0},{3,1},{4,6},{5,7},{6,4},{7,5},{8,10},{9,11},{10,... | collective-permute-start | bytes 98312 | tf_op jit(solution)/shard_map/ppermute | solution.py:458
  228.5 11.6 %collective-permute-start.13 = (f32[16,256]{1,0:T(8,128)S(1)}, f32[16,256]{1,0:T(8,128)S(1)}, u32[]{:S(2)}, u32[]{:S(2)}) collective-permute-start(f32[16,256]{1,0:T(8,128)S(1)} %slice_add_fusion.2), channel_id=1, source_target_pairs={{0,8},{1,9},{2,10},{3,11},{4,12},{5,13},{6,14},{7,15},{8,0},{9,1},... | collective-permute-start | bytes 49160 | tf_op jit(solution)/shard_map/ppermute | solution.py:458
  232.4 8.5 %copy-start.12 = (f32[16,256]{1,0:T(8,128)S(1)}, f32[16,256]{1,0:T(8,128)}, u32[]{:S(2)}) copy-start(f32[16,256]{1,0:T(8,128)} %get-tuple-element.14) | copy-start | bytes 49156
  232.5 8.5 %copy-start.13 = (s32[16]{0:T(128)S(1)}, s32[16]{0:T(128)}, u32[]{:S(2)}) copy-start(s32[16]{0:T(128)} %param.6) | copy-start | bytes 196
  232.5 8.5 %collective-permute-start.14 = (f32[16,256]{1,0:T(8,128)S(1)}, f32[16,256]{1,0:T(8,128)S(1)}, u32[]{:S(2)}, u32[]{:S(2)}) collective-permute-start(f32[16,256]{1,0:T(8,128)S(1)} %slice.29), channel_id=1, source_target_pairs={{0,1},{1,0},{2,3},{3,2},{4,5},{5,4},{6,7},{7,6},{8,9},{9,8},{10,11... | collective-permute-start | bytes 49160 | tf_op jit(solution)/shard_map/ppermute | solution.py:458
  (5 other events, 3.3 us)
where the time goes:
time: 243 us; the launch traced here: 242 us
  Pallas kernels  208 us (86%)
  starting transfers between devices  23 us (9%)
  waiting for transfers between devices  7.36 us (3%)
    pallas_call x1, Pallas kernels, rectangle(): pl.pallas_call(pair_kernel, out_shape=(shape(64), shape(32), shape(32), s...  207 us
    ppermute x15, starting transfers between devices, swap(): return lax.ppermute(array, 'frag', pairs)  23 us
    ppermute x15, waiting for transfers between devices, swap(): return lax.ppermute(array, 'frag', pairs)  7.36 us
  transfers between devices with their start and end apart: 15, of which 6 were waited for; matrix products, arithmetic and copies ran while one was open for 0% of the time, Pallas kernels for 0%

commit v1 on v0

--- a/solution.py
+++ b/solution.py
@@ -75,6 +75,12 @@
     def take_rows(h, at, count):
         return build.at[h][pl.ds(at, count, stride=16), :]
 
+    pick = lax.broadcasted_iota(jnp.int32, (128, 128), 0)
+
+    def spread(rows, lo, hi, scale):
+        sel = jnp.where((pick >= lo) & (pick <= hi), scale, 0.0)
+        return jnp.dot(rows, sel.astype(jnp.bfloat16), preferred_element_type=jnp.float32)
+
     lowest = None
     for i, blk in enumerate(f_blocks):
         loads[i].wait()
@@ -97,26 +103,17 @@
             for h in range(2):
                 feats = take_rows(h, lf, DEPTH).T
                 feats = jnp.concatenate([feats, jnp.zeros((128, 128 - DEPTH), jnp.float32)], axis=1)
-                lhs[pl.ds((i * 16 + lf) * CPF + 4 * h, 4), 0:CHUNK, :] = feats.astype(jnp.bfloat16).reshape(4, CHUNK, 128)
+                feats = feats.astype(jnp.bfloat16)
+                at = pl.ds((i * 16 + lf) * CPF + 4 * h, 4)
+                lhs[at, 0:CHUNK, :] = feats.reshape(4, CHUNK, 128)
+                rows_c[at] = spread(feats, 5, 7, 1.0).reshape(4, CHUNK, 128)
+                rows_s[at] = jnp.zeros((4, CHUNK, 128), jnp.float32)
             return 0
 
         lax.fori_loop(0, 16, one_row, 0, unroll=16)
     spare_lane = lax.broadcasted_iota(jnp.int32, (CHUNK, 128), 1)
     lhs[DUMMY, 0:CHUNK, :] = (spare_lane == 4).astype(jnp.float32).astype(jnp.bfloat16)
 
-    pick = lax.broadcasted_iota(jnp.int32, (128, 128), 0)
-
-    def spread(rows, lo, hi, scale):
-        sel = jnp.where((pick >= lo) & (pick <= hi), scale, 0.0)
-        return jnp.dot(rows, sel.astype(jnp.bfloat16), preferred_element_type=jnp.float32)
-
-    def one_spread(f, _):
-        value = spread(lhs[pl.ds(f * CPF, CPF), 0:CHUNK, :].reshape(AUX, 128), 5, 7, 1.0)
-        rows_c[pl.ds(f * CPF, CPF)] = value.reshape(CPF, CHUNK, 128)
-        rows_s[pl.ds(f * CPF, CPF)] = jnp.zeros((CPF, CHUNK, 128), jnp.float32)
-        return 0
-
-    lax.fori_loop(0, NF, one_spread, 0, unroll=16)
     rows_c[DUMMY] = jnp.zeros((CHUNK, 128), jnp.float32)
     rows_s[DUMMY] = jnp.zeros((CHUNK, 128), jnp.float32)
 
@@ -273,7 +270,7 @@
                 vals = tuple(jnp.where(a >= total, mark, v) for a, v in zip(at, vals))
                 return vals, total + jnp.where(listed == m.astype(jnp.float32), many, 0.0)
 
-            vals, total = lax.fori_loop(0, NF, scan, (vals, total), unroll=8)
+            vals, total = lax.fori_loop(0, NF, scan, (vals, total), unroll=16)
             vals = tuple(jnp.where(a >= total, -1.0, v) for a, v in zip(at, vals))
             total = jnp.floor((total + per_tile - 1.0) / per_tile) * per_tile
             return vals, times, total

time: 243 us -> 239 us (0.984)
  the two profiles are of different devices: /device:TPU:25 before, /device:TPU:0 now
where the time goes in v1:
time: 239 us; the launch traced here: 241 us
  Pallas kernels  169 us (71%)
  starting transfers between devices  60.7 us (25%)
  waiting for transfers between devices  8 us (3%)
    pallas_call x1, Pallas kernels, rectangle(): pl.pallas_call(pair_kernel, out_shape=(shape(64), shape(32), shape(32), s...  168 us
    ppermute x15, starting transfers between devices, swap(): return lax.ppermute(array, 'frag', pairs)  60.7 us
    ppermute x15, waiting for transfers between devices, swap(): return lax.ppermute(array, 'frag', pairs)  8 us
  transfers between devices with their start and end apart: 15, of which 5 were waited for; matrix products, arithmetic and copies ran while one was open for 0% of the time, Pallas kernels for 0%

profile of v1, /device:TPU:0, one launch (start us, length us, event | category | flops | bytes accessed | tf_op | source)
XLA Modules:
  0.0 241.2 jit_solution(9568999635881996131)
XLA Ops:
  0.0 1.6 shard_map.46.refs_0_
  1.6 3.1 %collective-permute-start.5 = (f32[96,256]{1,0:T(8,128)}, f32[96,256]{1,0:T(8,128)S(1)}, u32[]{:S(2)}, u32[]{:S(2)}) collective-permute-start(f32[96,256]{1,0:T(8,128)} %shard_map.46.refs_0_), channel_id=1, source_target_pairs={{0,4},{1,5},{2,6},{3,7},{4,0},{5,1},{6,2},{7,3},{8,12},{9,13},{10,... | collective-permute-start | bytes 294920 | tf_op jit(solution)/shard_map/ppermute | solution.py:455
  4.7 1.1 collective-permute-start.4
  5.8 3.9 %collective-permute-start.2 = (f32[96,256]{1,0:T(8,128)}, f32[96,256]{1,0:T(8,128)S(1)}, u32[]{:S(2)}, u32[]{:S(2)}) collective-permute-start(f32[96,256]{1,0:T(8,128)} %shard_map.46.refs_0_), channel_id=1, source_target_pairs={{0,16},{1,17},{2,18},{3,19},{4,20},{5,21},{6,22},{7,23},{8,24},{9,... | collective-permute-start | bytes 294920 | tf_op jit(solution)/shard_map/ppermute | solution.py:455
  9.7 0.7 collective-permute-start.1
  10.4 0.4 collective-permute-start
  10.8 0.2 collective-permute-done.4.refs_5_
  11.0 0.5 collective-permute-start.8
  11.5 1.7 collective-permute-done.2.refs_3_
  13.2 2.5 %collective-permute-done.1.refs_2_ = f32[96,256]{1,0:T(8,128)S(1)} collective-permute-done((f32[96,256]{1,0:T(8,128)}, f32[96,256]{1,0:T(8,128)S(1)}, u32[]{:S(2)}, u32[]{:S(2)}) %collective-permute-start.1) | collective-permute-done | bytes 98336 | tf_op jit(solution)/shard_map/ppermute | solution.py:455
  15.8 0.5 copy-done.5
  16.4 0.1 copy-done.6
  16.4 0.0 copy-done.8
  16.5 0.6 copy-done.9
  17.1 167.9 %shard_map.47 = (f32[64,256]{1,0:T(8,128)}, f32[32,256]{1,0:T(8,128)}, f32[32,256]{1,0:T(8,128)}, f32[32,256]{1,0:T(8,128)}, f32[16,256]{1,0:T(8,128)}, /*index=5*/f32[16,256]{1,0:T(8,128)}) custom-call(f32[96,256]{1,0:T(8,128)} %shard_map.46.refs_0_, f32[96,256]{1,0:T(8,128)} %copy-done.6, f32[96,256]{1,0:T(8,128)} %copy-done.5, f32[96,256]{1,0:T(8,128)} %copy-done.4, ...), custom_call_target="tpu_custom_call" | custom-call | tf_op jit(solution)/shard_map/pallas_call | solution.py:400
  185.0 29.2 %collective-permute-start.10 = (f32[64,256]{1,0:T(8,128)}, f32[64,256]{1,0:T(8,128)S(1)}, u32[]{:S(2)}, u32[]{:S(2)}) collective-permute-start(f32[64,256]{1,0:T(8,128)} %get-tuple-element.12), channel_id=1, source_target_pairs={{0,6},{1,7},{2,4},{3,5},{4,2},{5,3},{6,0},{7,1},{8,14},{9,15},{10,... | collective-permute-start | bytes 196616 | tf_op jit(solution)/shard_map/ppermute | solution.py:455
  214.2 15.9 %collective-permute-start.12 = (f32[32,256]{1,0:T(8,128)}, f32[32,256]{1,0:T(8,128)S(1)}, u32[]{:S(2)}, u32[]{:S(2)}) collective-permute-start(f32[32,256]{1,0:T(8,128)} %get-tuple-element.15), channel_id=1, source_target_pairs={{0,24},{1,25},{2,26},{3,27},{4,28},{5,29},{6,30},{7,31},{8,16},{9,... | collective-permute-start | bytes 98312 | tf_op jit(solution)/shard_map/ppermute | solution.py:455
  230.1 0.8 slice_add_fusion
  230.9 5.7 %collective-permute-start.11 = (f32[32,256]{1,0:T(8,128)S(1)}, f32[32,256]{1,0:T(8,128)S(1)}, u32[]{:S(2)}, u32[]{:S(2)}) collective-permute-start(f32[32,256]{1,0:T(8,128)S(1)} %slice_add_fusion), channel_id=1, source_target_pairs={{0,2},{1,3},{2,0},{3,1},{4,6},{5,7},{6,4},{7,5},{8,10},{9,11},{10,... | collective-permute-start | bytes 98312 | tf_op jit(solution)/shard_map/ppermute | solution.py:455
  236.6 0.1 collective-permute-start.13
  236.7 1.8 collective-permute-done.11
  238.6 0.1 collective-permute-start.14
  238.7 1.8 collective-permute-done.13
  240.5 0.7 fusion.3
  (41 shorter events, 0.1 us)
Async XLA Ops:
  1.6 8.1 %collective-permute-start.6 = (f32[96,256]{1,0:T(8,128)}, f32[96,256]{1,0:T(8,128)S(1)}, u32[]{:S(2)}, u32[]{:S(2)}) collective-permute-start(f32[96,256]{1,0:T(8,128)} %shard_map.46.refs_0_), channel_id=1, source_target_pairs={{0,1},{1,0},{2,3},{3,2},{4,5},{5,4},{6,7},{7,6},{8,9},{9,8},{10,11... | collective-permute-start | bytes 294920 | tf_op jit(solution)/shard_map/ppermute | solution.py:455
  1.6 8.9 %collective-permute-start.5 = (f32[96,256]{1,0:T(8,128)}, f32[96,256]{1,0:T(8,128)S(1)}, u32[]{:S(2)}, u32[]{:S(2)}) collective-permute-start(f32[96,256]{1,0:T(8,128)} %shard_map.46.refs_0_), channel_id=1, source_target_pairs={{0,4},{1,5},{2,6},{3,7},{4,0},{5,1},{6,2},{7,3},{8,12},{9,13},{10,... | collective-permute-start | bytes 294920 | tf_op jit(solution)/shard_map/ppermute | solution.py:455
  4.7 6.3 %collective-permute-start.4 = (f32[96,256]{1,0:T(8,128)}, f32[96,256]{1,0:T(8,128)S(1)}, u32[]{:S(2)}, u32[]{:S(2)}) collective-permute-start(f32[96,256]{1,0:T(8,128)} %shard_map.46.refs_0_), channel_id=1, source_target_pairs={{0,6},{1,7},{2,4},{3,5},{4,2},{5,3},{6,0},{7,1},{8,14},{9,15},{10,... | collective-permute-start | bytes 294920 | tf_op jit(solution)/shard_map/ppermute | solution.py:455
  5.8 5.2 %collective-permute-start.3 = (f32[96,256]{1,0:T(8,128)}, f32[96,256]{1,0:T(8,128)S(1)}, u32[]{:S(2)}, u32[]{:S(2)}) collective-permute-start(f32[96,256]{1,0:T(8,128)} %shard_map.46.refs_0_), channel_id=1, source_target_pairs={{0,2},{1,3},{2,0},{3,1},{4,6},{5,7},{6,4},{7,5},{8,10},{9,11},{10,... | collective-permute-start | bytes 294920 | tf_op jit(solution)/shard_map/ppermute | solution.py:455
  5.8 7.4 %collective-permute-start.2 = (f32[96,256]{1,0:T(8,128)}, f32[96,256]{1,0:T(8,128)S(1)}, u32[]{:S(2)}, u32[]{:S(2)}) collective-permute-start(f32[96,256]{1,0:T(8,128)} %shard_map.46.refs_0_), channel_id=1, source_target_pairs={{0,16},{1,17},{2,18},{3,19},{4,20},{5,21},{6,22},{7,23},{8,24},{9,... | collective-permute-start | bytes 294920 | tf_op jit(solution)/shard_map/ppermute | solution.py:455
  9.7 6.1 %copy-start = (f32[96,256]{1,0:T(8,128)}, f32[96,256]{1,0:T(8,128)S(1)}, u32[]{:S(2)}) copy-start(f32[96,256]{1,0:T(8,128)S(1)} %collective-permute-done.6.refs_7_) | copy-start | bytes 294916
  9.7 6.0 %collective-permute-start.1 = (f32[96,256]{1,0:T(8,128)}, f32[96,256]{1,0:T(8,128)S(1)}, u32[]{:S(2)}, u32[]{:S(2)}) collective-permute-start(f32[96,256]{1,0:T(8,128)} %shard_map.46.refs_0_), channel_id=1, source_target_pairs={{0,24},{1,25},{2,26},{3,27},{4,28},{5,29},{6,30},{7,31},{8,16},{9,... | collective-permute-start | bytes 294920 | tf_op jit(solution)/shard_map/ppermute | solution.py:455
  10.4 5.4 %copy-start.1 = (f32[96,256]{1,0:T(8,128)}, f32[96,256]{1,0:T(8,128)S(1)}, u32[]{:S(2)}) copy-start(f32[96,256]{1,0:T(8,128)S(1)} %collective-permute-done.5.refs_6_) | copy-start | bytes 294916
  10.4 5.3 %collective-permute-start = (f32[96,256]{1,0:T(8,128)}, f32[96,256]{1,0:T(8,128)S(1)}, u32[]{:S(2)}, u32[]{:S(2)}) collective-permute-start(f32[96,256]{1,0:T(8,128)} %shard_map.46.refs_0_), channel_id=1, source_target_pairs={{0,8},{1,9},{2,10},{3,11},{4,12},{5,13},{6,14},{7,15},{8,0},{9,1},... | collective-permute-start | bytes 294920 | tf_op jit(solution)/shard_map/ppermute | solution.py:455
  11.0 4.8 %copy-start.2 = (f32[96,256]{1,0:T(8,128)}, f32[96,256]{1,0:T(8,128)S(1)}, u32[]{:S(2)}) copy-start(f32[96,256]{1,0:T(8,128)S(1)} %collective-permute-done.4.refs_5_) | copy-start | bytes 294916
  11.0 4.7 %collective-permute-start.9 = (f32[96,256]{1,0:T(8,128)S(1)}, f32[96,256]{1,0:T(8,128)S(1)}, u32[]{:S(2)}, u32[]{:S(2)}) collective-permute-start(f32[96,256]{1,0:T(8,128)S(1)} %collective-permute-done.5.refs_6_), channel_id=1, source_target_pairs={{0,1},{1,0},{2,3},{3,2},{4,5},{5,4},{6,7},{7,6},{8,9},{9,8},{10,11... | collective-permute-start | bytes 294920 | tf_op jit(solution)/shard_map/ppermute | solution.py:455
  11.0 4.8 %copy-start.3 = (f32[96,256]{1,0:T(8,128)}, f32[96,256]{1,0:T(8,128)S(1)}, u32[]{:S(2)}) copy-start(f32[96,256]{1,0:T(8,128)S(1)} %collective-permute-done.3.refs_4_) | copy-start | bytes 294916
  11.0 4.7 %collective-permute-start.8 = (f32[96,256]{1,0:T(8,128)S(1)}, f32[96,256]{1,0:T(8,128)S(1)}, u32[]{:S(2)}, u32[]{:S(2)}) collective-permute-start(f32[96,256]{1,0:T(8,128)S(1)} %collective-permute-done.4.refs_5_), channel_id=1, source_target_pairs={{0,1},{1,0},{2,3},{3,2},{4,5},{5,4},{6,7},{7,6},{8,9},{9,8},{10,11... | collective-permute-start | bytes 294920 | tf_op jit(solution)/shard_map/ppermute | solution.py:455
  13.2 2.6 %copy-start.4 = (f32[96,256]{1,0:T(8,128)}, f32[96,256]{1,0:T(8,128)S(1)}, u32[]{:S(2)}) copy-start(f32[96,256]{1,0:T(8,128)S(1)} %collective-permute-done.2.refs_3_) | copy-start | bytes 294916
  13.2 2.6 %collective-permute-start.7 = (f32[96,256]{1,0:T(8,128)S(1)}, f32[96,256]{1,0:T(8,128)S(1)}, u32[]{:S(2)}, u32[]{:S(2)}) collective-permute-start(f32[96,256]{1,0:T(8,128)S(1)} %collective-permute-done.3.refs_4_), channel_id=1, source_target_pairs={{0,1},{1,0},{2,3},{3,2},{4,5},{5,4},{6,7},{7,6},{8,9},{9,8},{10,11... | collective-permute-start | bytes 294920 | tf_op jit(solution)/shard_map/ppermute | solution.py:455
  185.0 45.1 %collective-permute-start.10 = (f32[64,256]{1,0:T(8,128)}, f32[64,256]{1,0:T(8,128)S(1)}, u32[]{:S(2)}, u32[]{:S(2)}) collective-permute-start(f32[64,256]{1,0:T(8,128)} %get-tuple-element.12), channel_id=1, source_target_pairs={{0,6},{1,7},{2,4},{3,5},{4,2},{5,3},{6,0},{7,1},{8,14},{9,15},{10,... | collective-permute-start | bytes 196616 | tf_op jit(solution)/shard_map/ppermute | solution.py:455
  214.2 22.4 %collective-permute-start.12 = (f32[32,256]{1,0:T(8,128)}, f32[32,256]{1,0:T(8,128)S(1)}, u32[]{:S(2)}, u32[]{:S(2)}) collective-permute-start(f32[32,256]{1,0:T(8,128)} %get-tuple-element.15), channel_id=1, source_target_pairs={{0,24},{1,25},{2,26},{3,27},{4,28},{5,29},{6,30},{7,31},{8,16},{9,... | collective-permute-start | bytes 98312 | tf_op jit(solution)/shard_map/ppermute | solution.py:455
  230.1 6.5 %copy-start.11 = (f32[16,256]{1,0:T(8,128)S(1)}, f32[16,256]{1,0:T(8,128)}, u32[]{:S(2)}) copy-start(f32[16,256]{1,0:T(8,128)} %get-tuple-element.16) | copy-start | bytes 49156
  230.9 7.6 %copy-start.10 = (f32[32,256]{1,0:T(8,128)S(1)}, f32[32,256]{1,0:T(8,128)}, u32[]{:S(2)}) copy-start(f32[32,256]{1,0:T(8,128)} %get-tuple-element.11) | copy-start | bytes 98308
  230.9 7.6 %collective-permute-start.11 = (f32[32,256]{1,0:T(8,128)S(1)}, f32[32,256]{1,0:T(8,128)S(1)}, u32[]{:S(2)}, u32[]{:S(2)}) collective-permute-start(f32[32,256]{1,0:T(8,128)S(1)} %slice_add_fusion), channel_id=1, source_target_pairs={{0,2},{1,3},{2,0},{3,1},{4,6},{5,7},{6,4},{7,5},{8,10},{9,11},{10,... | collective-permute-start | bytes 98312 | tf_op jit(solution)/shard_map/ppermute | solution.py:455
  236.6 3.8 %collective-permute-start.13 = (f32[16,256]{1,0:T(8,128)S(1)}, f32[16,256]{1,0:T(8,128)S(1)}, u32[]{:S(2)}, u32[]{:S(2)}) collective-permute-start(f32[16,256]{1,0:T(8,128)S(1)} %slice_add_fusion.2), channel_id=1, source_target_pairs={{0,8},{1,9},{2,10},{3,11},{4,12},{5,13},{6,14},{7,15},{8,0},{9,1},... | collective-permute-start | bytes 49160 | tf_op jit(solution)/shard_map/ppermute | solution.py:455
  238.5 1.9 copy-start.12
  238.6 1.9 copy-start.13
  238.6 1.9 collective-permute-start.14
  (5 other events, 3.3 us)
